TPU v7x, 32 devices: a whole 2x2x4 slice. The times are simulated.
32 devices in a mesh: row: 4 (over y, x), col: 8 (over z, core).
Axes of the slice: x: 2, y: 2, z: 4, core: 2. Of those that a mesh axis runs over, the one named last changes fastest.
Arguments:
- amplitudes: bfloat16 [8192, 1024], P('col', 'row'), may hold values from -6 to 6
- integrals: bfloat16 [1024, 4096], P('col', 'row'), may hold values from -0.5 to 0.5
- sym_mask: int32 [8, 32], replicated, may hold values from 0 to 1, as said below
Outputs:
- ladder: bfloat16 [8192, 4096], P('col', 'row')
Inputs may be any that keep to these rules, and one draw needn't show every extreme that they name: sym_mask[k, a] is 1 exactly when cd tile k and ab tile a carry the same one of 8 irreducible representations; among the 8 ab tiles of one index of row, at most 2 carry the same representation.
All inputs are finite; a program needn't handle non-finite values.
Results may differ from a plain program's by a relative error of at most 0.001.
Values may be sent and summed in bfloat16 or wider, within the bound.
A program may use at most 64 MiB of HBM per device.

v0:
```python
import jax
import jax.numpy as jnp
from jax import lax
from jax.sharding import PartitionSpec as P

TILE = 128
AB_TILES = 8


def shards(amplitudes, integrals, sym_mask):
    row_index = lax.axis_index("row")
    col_index = lax.axis_index("col")
    own_mask = lax.dynamic_slice(sym_mask, (col_index, row_index * AB_TILES), (1, AB_TILES))
    column_mask = jnp.repeat(own_mask[0], TILE).astype(jnp.bfloat16)
    masked = integrals * column_mask[None, :]
    whole_amps = lax.all_gather(amplitudes, "row", axis=1, tiled=True)
    total = jnp.dot(
        whole_amps,
        lax.all_gather(masked, "col", axis=0, tiled=True),
        preferred_element_type=jnp.float32,
    )
    return total.astype(jnp.bfloat16)


def solution(mesh):
    placed = (P("col", "row"), P("col", "row"), P())
    return jax.shard_map(
        shards, mesh=mesh, in_specs=placed, out_specs=P("col", "row"), check_vma=False
    )
```

profile of v0, /device:TPU:0, one launch (start us, length us, event | category | flops | bytes accessed | tf_op | source)
XLA Modules:
  0.0 91.8 jit_solution(10614195048144689264)
XLA Ops:
  6.5 0.0 all-gather.5.cloned.1.call-start
  6.5 0.7 all-gather.5.cloned.1.call-update
  7.3 0.0 all-gather.3.cloned.1.call-start
  7.3 0.8 convert_bitcast_fusion.1
  8.1 0.1 broadcast_bitcast_fusion
  8.2 1.7 %broadcast_multiply_fusion = bf16[128,1024]{1,0:T(8,128)(2,1)} fusion(bf16[128,1024]{1,0:T(8,128)(2,1)} %param.4, bf16[1024]{0:T(1024)(128)(2,1)S(1)} %broadcast_bitcast_fusion), kind=kLoop, calls=%fused_computation.1 | loop fusion | flops 131072 | bytes 526336 | tf_op jit(solution)/shard_map/mul | solution.py:15
  9.8 0.0 all-gather.3.cloned.1.call-update
  9.8 37.2 %all-gather.5.cloned.1.call-done = bf16[1024,1024]{1,0:T(8,128)(2,1)} async-done(((bf16[1024,256]{1,0:T(8,128)(2,1)}), bf16[1024,1024]{1,0:T(8,128)(2,1)}) %all-gather.5.cloned.1.call-update) | async-done | bytes 2097168 | tf_op jit(solution)/shard_map/all_gather | solution.py:16
  47.1 30.7 %all-gather.3.cloned.1.call-done = bf16[1024,1024]{1,0:T(8,128)(2,1)} async-done(((bf16[128,1024]{1,0:T(8,128)(2,1)}), bf16[1024,1024]{1,0:T(8,128)(2,1)}) %all-gather.3.cloned.1.call-update) | async-done | bytes 2097168 | tf_op jit(solution)/shard_map/all_gather | solution.py:19
  77.8 4.6 %convert_bitcast_fusion = bf16[1024,1024]{0,1:T(8,128)(2,1)S(1)} fusion(bf16[1024,1024]{1,0:T(8,128)(2,1)} %all-gather.3.cloned.1.call-done, bf16[1024,1024]{1,0:T(8,128)(2,1)} %all-gather.5.cloned.1.call-done), kind=kOutput, calls=%fused_computation | convolution fusion | flops 2148532224 | bytes 6291456 | tf_op jit(solution)/shard_map/dot_general | solution.py:17
  82.4 2.6 %copy.4 = bf16[1024,1024]{1,0:T(8,128)(2,1)} copy(bf16[1024,1024]{0,1:T(8,128)(2,1)S(1)} %convert_bitcast_fusion) | data formatting | bytes 4194304 | tf_op jit(solution)/shard_map/convert_element_type | solution.py:22
Async XLA Ops:
  6.5 40.5 %all-gather.5.cloned.1.call-start = ((), (), s32[]{:S(2)}) async-start(), calls=%async_computation.1 | async-start | bytes 2621440 | tf_op jit(solution)/shard_map/all_gather | solution.py:16
  7.3 70.6 %all-gather.3.cloned.1.call-start = ((), (), s32[]{:S(2)}) async-start(), calls=%async_computation | async-start | bytes 2359296 | tf_op jit(solution)/shard_map/all_gather | solution.py:19
Sparse Core Ops, SparseCore 0:
  9.2 37.8 all-gather.4
  48.7 29.0 all-gather.2
where the time goes:
time: 92 us; the launch traced here: 91.8 us
  waiting for transfers between devices  68.7 us (75%)
  between operations  13.4 us (15%)
  matrix products  4.6 us (5%)
  local copies, waits for them, and re-layouts  2.64 us (3%)
  other arithmetic  2.44 us (3%)
    all_gather x1, waiting for transfers between devices, shards(): whole_amps = lax.all_gather(amplitudes, 'row', axis=1, tiled=True)  37.2 us
    all_gather x1, waiting for transfers between devices, shards(): lax.all_gather(masked, 'col', axis=0, tiled=True)  30.7 us
    dot_general x1, matrix products, shards(): jnp.dot(whole_amps, lax.all_gather(masked, 'col', axis=0, tiled=True), pr...  4.6 us
    convert_element_type x1, local copies, waits for them, and re-layouts, shards(): return total.astype(jnp.bfloat16)  2.56 us
  transfers between devices with their start and end apart: 2, of which 2 were waited for; matrix products, arithmetic and copies ran while one was open for 3% of the time, Pallas kernels for 0%

commit v1 on v0

v1 whole, which is shorter than its diff:
```python
import functools

import jax
import jax.numpy as jnp
from jax import lax
from jax.experimental import pallas as pl
from jax.experimental.pallas import tpu as pltpu
from jax.sharding import PartitionSpec as P

TILE = 128
SLOTS = 2
CHUNKS = 8
WINDOW = 2
MESH = pl.DeviceIdType.MESH


def kernel(n_row, n_col, amps, ints, mask, out, rows_all, dense, comp, ints_v, out_v,
           local_sem, out_sem, own_send, fwd_send, amp_recv, v_send, v_recv, s_send):
    ni, nj = 2, n_row // 2
    row, col = lax.axis_index("row"), lax.axis_index("col")
    i, j = row // nj, row % nj
    n_ij, n_cd = amps.shape
    n_ab = ints.shape[1]
    n_tiles = n_ab // TILE
    step_rows = n_ij // CHUNKS

    own_copy = pltpu.make_async_copy(
        amps, rows_all.at[:, pl.ds(pl.multiple_of(row * n_cd, n_cd), n_cd)], local_sem.at[0])
    ints_copy = pltpu.make_async_copy(ints, ints_v, local_sem.at[1])
    ints_copy.start()
    own_copy.start()

    same_i = [i * nj + (j + d) % nj for d in range(1, nj)]
    same_j = [((i + d) % ni) * nj + j for d in range(1, ni)]
    near = same_i + same_j
    peers = [(col + 2 * d) % n_col for d in range(1, n_col // 2)]
    sibling = col + 1 - 2 * (col % 2)

    barrier = pltpu.get_barrier_semaphore()
    for peer in near:
        pl.semaphore_signal(barrier, inc=1, device_id={"row": peer}, device_id_type=MESH)
    for peer in peers + [sibling]:
        pl.semaphore_signal(barrier, inc=1, device_id={"col": peer}, device_id_type=MESH)
    pl.semaphore_wait(barrier, len(near) + len(peers) + 1)

    def part(source, c):
        return rows_all.at[pl.ds(c * step_rows, step_rows),
                           pl.ds(pl.multiple_of(source * n_cd, n_cd), n_cd)]

    def own(c, d):
        return pltpu.make_async_remote_copy(
            src_ref=amps.at[pl.ds(c * step_rows, step_rows)], dst_ref=part(row, c),
            send_sem=own_send.at[d, c], recv_sem=amp_recv.at[row, c],
            device_id={"row": near[d]}, device_id_type=MESH)

    def forwards(c):
        sources, targets = (same_i, same_j) if c % 2 == 0 else (same_j, same_i)
        return [[pltpu.make_async_remote_copy(
            src_ref=part(source, c), dst_ref=part(source, c),
            send_sem=fwd_send.at[a * len(targets) + b, c], recv_sem=amp_recv.at[source, c],
            device_id={"row": target}, device_id_type=MESH)
            for b, target in enumerate(targets)] for a, source in enumerate(sources)]

    def arrive(source, c):
        pltpu.make_async_copy(part(source, c), part(source, c), amp_recv.at[source, c]).wait()

    def start_own(c):
        for d in range(len(near)):
            own(c, d).start()

    for c in range(WINDOW):
        start_own(c)

    def slot_weights(k):
        seen = jnp.int32(0)
        weights = []
        for t in range(n_tiles):
            m = mask[k, row * n_tiles + t]
            weights.append(((m * (1 - jnp.minimum(seen, 1))).astype(jnp.float32),
                            (m * jnp.minimum(seen, 1)).astype(jnp.float32)))
            seen = seen + m
        return weights

    ints_copy.wait()
    weights = slot_weights(col)
    for s in range(SLOTS):
        total = jnp.zeros((TILE, TILE), jnp.float32)
        for t in range(n_tiles):
            total += ints_v[:, t * TILE:(t + 1) * TILE].astype(jnp.float32) * weights[t][s]
        comp[col, s] = total.astype(jnp.bfloat16)

    def v_copy(d):
        return pltpu.make_async_remote_copy(
            src_ref=comp.at[col], dst_ref=comp.at[col], send_sem=v_send.at[d], recv_sem=v_recv.at[col],
            device_id={"col": peers[d]}, device_id_type=MESH)

    def sibling_copy(d):
        source = col if d == 0 else peers[d - 1]
        return pltpu.make_async_remote_copy(
            src_ref=comp.at[source], dst_ref=comp.at[source], send_sem=s_send.at[d],
            recv_sem=v_recv.at[source], device_id={"col": sibling}, device_id_type=MESH)

    def v_arrive(source):
        pltpu.make_async_copy(comp.at[source], comp.at[source], v_recv.at[source]).wait()

    for d in range(len(peers)):
        v_copy(d).start()
    sibling_copy(0).start()

    def build_dense():
        def one(k, carry):
            first = comp[k, 0].astype(jnp.float32)
            second = comp[k, 1].astype(jnp.float32)
            w = slot_weights(k)
            for t in range(n_tiles):
                dense[pl.ds(pl.multiple_of(k * TILE, TILE), TILE), t * TILE:(t + 1) * TILE] = (
                    first * w[t][0] + second * w[t][1]).astype(jnp.bfloat16)
            return carry
        lax.fori_loop(0, n_col, one, 0)

    def out_copy(c):
        span = pl.ds(c * step_rows, step_rows)
        return pltpu.make_async_copy(out_v.at[span], out.at[span], out_sem.at[c])

    def multiply(c):
        corner = [(i2, j2) for i2 in range(1, ni) for j2 in range(1, nj)]
        for di, dj in corner:
            arrive(((i + di) % ni) * nj + (j + dj) % nj, c)
        span = slice(c * step_rows, (c + 1) * step_rows)
        width = 2 * TILE
        for at in range(0, n_ab, width):
            out_v[span, at:at + width] = jnp.dot(
                rows_all[span, :], dense[:, at:at + width],
                preferred_element_type=jnp.float32).astype(jnp.bfloat16)
        out_copy(c).start()

    def take(c):
        copies = forwards(c)
        sources, others = (same_i, same_j) if c % 2 == 0 else (same_j, same_i)
        for source, group in zip(sources, copies):
            arrive(source, c)
            for copy in group:
                copy.start()
        for source in others:
            arrive(source, c)

    lag = 3
    for c in range(CHUNKS):
        if c + WINDOW < CHUNKS:
            start_own(c + WINDOW)
        take(c)
        if c == 2:
            for d in range(len(peers)):
                v_arrive(peers[d])
                sibling_copy(d + 1).start()
        if c == 3:
            own_copy.wait()
            v_arrive(sibling)
            for d in range(len(peers)):
                v_arrive((sibling + 2 * (d + 1)) % n_col)
            build_dense()
        if c >= 4:
            multiply(c - 4)
    for c in range(CHUNKS - 4, CHUNKS):
        multiply(c)

    for c in range(CHUNKS):
        for d in range(len(near)):
            own(c, d).wait_send()
        for group in forwards(c):
            for copy in group:
                copy.wait_send()
    for d in range(len(peers)):
        v_copy(d).wait_send()
    for d in range(len(peers) + 1):
        sibling_copy(d).wait_send()
    for c in range(CHUNKS):
        out_copy(c).wait()


def shards(n_row, n_col, amplitudes, integrals, sym_mask):
    n_ij, n_cd = amplitudes.shape
    n_ab = integrals.shape[1]
    near = 1 + n_row // 2 - 1
    dma = pltpu.SemaphoreType.DMA
    return pl.pallas_call(
        functools.partial(kernel, n_row, n_col),
        out_shape=jax.ShapeDtypeStruct((n_ij, n_ab), jnp.bfloat16),
        in_specs=[pl.BlockSpec(memory_space=pl.ANY), pl.BlockSpec(memory_space=pl.ANY),
                  pl.BlockSpec(memory_space=pltpu.SMEM)],
        out_specs=pl.BlockSpec(memory_space=pl.ANY),
        scratch_shapes=[
            pltpu.VMEM((n_ij, n_cd * n_row), jnp.bfloat16),
            pltpu.VMEM((n_col * TILE, n_ab), jnp.bfloat16),
            pltpu.VMEM((n_col, SLOTS, TILE, TILE), jnp.bfloat16),
            pltpu.VMEM((TILE, n_ab), jnp.bfloat16),
            pltpu.VMEM((n_ij, n_ab), jnp.bfloat16),
            dma((2,)),
            dma((CHUNKS,)),
            dma((near, CHUNKS)),
            dma((max(n_row // 2 - 1, 1), CHUNKS)),
            dma((n_row, CHUNKS)),
            dma((n_col // 2,)),
            dma((n_col,)),
            dma((n_col // 2,)),
        ],
        cost_estimate=pl.CostEstimate(
            flops=2 * n_ij * n_ab * n_cd * n_row, bytes_accessed=6 * n_ij * n_ab, transcendentals=0),
        compiler_params=pltpu.CompilerParams(
            collective_id=0, has_side_effects=True, vmem_limit_bytes=48 * 1024 * 1024),
    )(amplitudes, integrals, sym_mask)


def solution(mesh):
    placed = (P("col", "row"), P("col", "row"), P())
    return jax.shard_map(
        functools.partial(shards, mesh.shape["row"], mesh.shape["col"]),
        mesh=mesh, in_specs=placed, out_specs=P("col", "row"), check_vma=False,
    )
```

time: 92 us -> 33.1 us (0.36)
  waiting for transfers between devices: 68.7 us -> 0 us
  Pallas kernels: 0 us -> 28.9 us
  between operations: 13.4 us -> 0.01 us
  matrix products: 4.6 us -> 0 us
  other arithmetic: 2.44 us -> 0 us
  local copies, waits for them, and re-layouts: 2.64 us -> 4 us
    all_gather x2 -> x0, waiting for transfers between devices: 68 us -> none  [the longest x1 37.2 us: shards(): whole_amps = lax.all_gather(amplitudes, 'row', axis=1, tiled=True)]
    pallas_call x0 -> x1, Pallas kernels: none -> 28.9 us  [shards(): pl.pallas_call(functools.partial(kernel, n_row, n_col), out_shape=jax.Sha...]
    dot_general x1 -> x0, matrix products: 4.6 us -> none  [shards(): jnp.dot(whole_amps, lax.all_gather(masked, 'col', axis=0, tiled=True), pr...]
    unnamed x0 -> x7, local copies, waits for them, and re-layouts: none -> 4 us
    convert_element_type x2 -> x0, local copies, waits for them, and re-layouts: 2.64 us -> none  [the longest x1 2.56 us: shards(): return total.astype(jnp.bfloat16)]
    mul x1 -> x0, other arithmetic: 1.67 us -> none  [shards(): masked = integrals * column_mask[None, :]]
  transfers between devices with their start and end apart: 2 -> 0, of which waited for: 2 -> 0; matrix products, arithmetic and copies ran while one was open for 3% -> 0% of each run, Pallas kernels for 0% -> 0%
where the time goes in v1:
time: 33.1 us; the launch traced here: 32.9 us
  Pallas kernels  28.9 us (87%)
  local copies, waits for them, and re-layouts  4 us (12%)
    pallas_call x1, Pallas kernels, shards(): pl.pallas_call(functools.partial(kernel, n_row, n_col), out_shape=jax.Sha...  28.9 us
    unnamed x7, local copies, waits for them, and re-layouts  4 us

profile of v1, /device:TPU:0, one launch (start us, length us, event | category | flops | bytes accessed | tf_op | source)
XLA Modules:
  0.0 32.9 jit_solution(6891167738870164693)
XLA Ops:
  0.0 0.0 copy-start
  0.0 1.0 %copy-done = bf16[1024,256]{1,0:T(8,128)(2,1)S(1)} copy-done((bf16[1024,256]{1,0:T(8,128)(2,1)S(1)}, bf16[1024,256]{1,0:T(8,128)(2,1)}, u32[]{:S(2)}) %copy-start) | copy-done | bytes 524312
  1.0 0.0 copy-start.1
  1.0 0.9 %copy-done.1 = bf16[128,1024]{1,0:T(8,128)(2,1)S(1)} copy-done((bf16[128,1024]{1,0:T(8,128)(2,1)S(1)}, bf16[128,1024]{1,0:T(8,128)(2,1)}, u32[]{:S(2)}) %copy-start.1) | copy-done | bytes 262168
  2.0 0.0 copy-start.2
  2.0 0.7 %copy-done.2 = s32[8,32]{1,0:T(8,128)S(1)} copy-done((s32[8,32]{1,0:T(8,128)S(1)}, s32[8,32]{1,0:T(8,128)}, u32[]{:S(2)}) %copy-start.2) | copy-done | bytes 1048
  2.7 28.9 %shard_map.37 = bf16[1024,1024]{1,0:T(8,128)(2,1)S(1)} custom-call(bf16[1024,256]{1,0:T(8,128)(2,1)S(1)} %copy-done, bf16[128,1024]{1,0:T(8,128)(2,1)S(1)} %copy-done.1, s32[8,32]{1,0:T(8,128)S(1)} %copy-done.2), custom_call_target="tpu_custom_call" | custom-call | flops 2147483648 | bytes 6291456 | tf_op jit(solution)/shard_map/pallas_call | solution.py:186
  31.5 1.3 %copy.5 = bf16[1024,1024]{1,0:T(8,128)(2,1)} copy(bf16[1024,1024]{1,0:T(8,128)(2,1)S(1)} %shard_map.37) | data formatting | bytes 4194304
Async XLA Ops:
  0.0 1.0 %copy-start = (bf16[1024,256]{1,0:T(8,128)(2,1)S(1)}, bf16[1024,256]{1,0:T(8,128)(2,1)}, u32[]{:S(2)}) copy-start(bf16[1024,256]{1,0:T(8,128)(2,1)} %amps.1) | copy-start | bytes 1572868
  1.0 0.9 %copy-start.1 = (bf16[128,1024]{1,0:T(8,128)(2,1)S(1)}, bf16[128,1024]{1,0:T(8,128)(2,1)}, u32[]{:S(2)}) copy-start(bf16[128,1024]{1,0:T(8,128)(2,1)} %ints.1) | copy-start | bytes 786436
  2.0 0.7 %copy-start.2 = (s32[8,32]{1,0:T(8,128)S(1)}, s32[8,32]{1,0:T(8,128)}, u32[]{:S(2)}) copy-start(s32[8,32]{1,0:T(8,128)} %mask.1) | copy-start | bytes 3076

commit v2 on v1

--- a/solution.py
+++ b/solution.py
@@ -10,12 +10,12 @@
 TILE = 128
 SLOTS = 2
 CHUNKS = 8
-WINDOW = 2
+WINDOW = 4
 MESH = pl.DeviceIdType.MESH
 
 
-def kernel(n_row, n_col, amps, ints, mask, out, rows_all, dense, comp, ints_v, out_v,
-           local_sem, out_sem, own_send, fwd_send, amp_recv, v_send, v_recv, s_send):
+def kernel(n_row, n_col, amps, ints, mask_hbm, out, rows_all, dense, comp, ints_v, out_v, mask,
+           ready_z, ready_core, local_sem, out_sem, own_send, fwd_send, amp_recv, v_send, v_recv, s_send):
     ni, nj = 2, n_row // 2
     row, col = lax.axis_index("row"), lax.axis_index("col")
     i, j = row // nj, row % nj
@@ -27,21 +27,33 @@
     own_copy = pltpu.make_async_copy(
         amps, rows_all.at[:, pl.ds(pl.multiple_of(row * n_cd, n_cd), n_cd)], local_sem.at[0])
     ints_copy = pltpu.make_async_copy(ints, ints_v, local_sem.at[1])
-    ints_copy.start()
-    own_copy.start()
+    mask_copy = pltpu.make_async_copy(mask_hbm, mask, local_sem.at[2])
 
     same_i = [i * nj + (j + d) % nj for d in range(1, nj)]
     same_j = [((i + d) % ni) * nj + j for d in range(1, ni)]
     near = same_i + same_j
-    peers = [(col + 2 * d) % n_col for d in range(1, n_col // 2)]
-    sibling = col + 1 - 2 * (col % 2)
+    n_z = n_col // 2
+    z, core = col // 2, col % 2
+    peers = [(z + d) % n_z for d in range(1, n_z)]
+    sibling = col + 1 - 2 * core
 
     barrier = pltpu.get_barrier_semaphore()
     for peer in near:
         pl.semaphore_signal(barrier, inc=1, device_id={"row": peer}, device_id_type=MESH)
-    for peer in peers + [sibling]:
-        pl.semaphore_signal(barrier, inc=1, device_id={"col": peer}, device_id_type=MESH)
-    pl.semaphore_wait(barrier, len(near) + len(peers) + 1)
+    for peer in peers:
+        @pl.when(peer > z)
+        def _():
+            pl.semaphore_signal(
+                barrier, inc=1, device_id={"col": 2 * peer + core}, device_id_type=MESH)
+
+    @pl.when(core == 0)
+    def _():
+        pl.semaphore_signal(barrier, inc=1, device_id={"col": sibling}, device_id_type=MESH)
+
+    ints_copy.start()
+    mask_copy.start()
+    own_copy.start()
+    pl.semaphore_wait(barrier, len(near) + z + core)
 
     def part(source, c):
         return rows_all.at[pl.ds(c * step_rows, step_rows),
@@ -81,7 +93,18 @@
             seen = seen + m
         return weights
 
+    for peer in peers:
+        @pl.when(peer < z)
+        def _():
+            pl.semaphore_signal(
+                ready_z.at[z], inc=1, device_id={"col": 2 * peer + core}, device_id_type=MESH)
+
+    @pl.when(core == 1)
+    def _():
+        pl.semaphore_signal(ready_core, inc=1, device_id={"col": sibling}, device_id_type=MESH)
+
     ints_copy.wait()
+    mask_copy.wait()
     weights = slot_weights(col)
     for s in range(SLOTS):
         total = jnp.zeros((TILE, TILE), jnp.float32)
@@ -92,10 +115,10 @@
     def v_copy(d):
         return pltpu.make_async_remote_copy(
             src_ref=comp.at[col], dst_ref=comp.at[col], send_sem=v_send.at[d], recv_sem=v_recv.at[col],
-            device_id={"col": peers[d]}, device_id_type=MESH)
+            device_id={"col": 2 * peers[d] + core}, device_id_type=MESH)
 
     def sibling_copy(d):
-        source = col if d == 0 else peers[d - 1]
+        source = col if d == 0 else 2 * peers[d - 1] + core
         return pltpu.make_async_remote_copy(
             src_ref=comp.at[source], dst_ref=comp.at[source], send_sem=s_send.at[d],
             recv_sem=v_recv.at[source], device_id={"col": sibling}, device_id_type=MESH)
@@ -103,9 +126,6 @@
     def v_arrive(source):
         pltpu.make_async_copy(comp.at[source], comp.at[source], v_recv.at[source]).wait()
 
-    for d in range(len(peers)):
-        v_copy(d).start()
-    sibling_copy(0).start()
 
     def build_dense():
         def one(k, carry):
@@ -144,24 +164,38 @@
         for source in others:
             arrive(source, c)
 
-    lag = 3
     for c in range(CHUNKS):
         if c + WINDOW < CHUNKS:
             start_own(c + WINDOW)
         take(c)
-        if c == 2:
-            for d in range(len(peers)):
-                v_arrive(peers[d])
+        if c == 0:
+            for d, peer in enumerate(peers):
+                @pl.when(peer > z)
+                def _():
+                    pl.semaphore_wait(ready_z.at[peer], 1)
+                v_copy(d).start()
+
+            @pl.when(core == 0)
+            def _():
+                pl.semaphore_wait(ready_core, 1)
+            sibling_copy(0).start()
+        if c == 3:
+            for d, peer in enumerate(peers):
+                v_arrive(2 * peer + core)
                 sibling_copy(d + 1).start()
-        if c == 3:
+        if c == 5:
             own_copy.wait()
             v_arrive(sibling)
-            for d in range(len(peers)):
-                v_arrive((sibling + 2 * (d + 1)) % n_col)
+            for peer in peers:
+                v_arrive(2 * peer + 1 - core)
             build_dense()
-        if c >= 4:
-            multiply(c - 4)
-    for c in range(CHUNKS - 4, CHUNKS):
+            multiply(0)
+        if c == 6:
+            multiply(1)
+            multiply(2)
+        if c == 7:
+            multiply(3)
+    for c in range(4, CHUNKS):
         multiply(c)
 
     for c in range(CHUNKS):
@@ -186,8 +220,7 @@
     return pl.pallas_call(
         functools.partial(kernel, n_row, n_col),
         out_shape=jax.ShapeDtypeStruct((n_ij, n_ab), jnp.bfloat16),
-        in_specs=[pl.BlockSpec(memory_space=pl.ANY), pl.BlockSpec(memory_space=pl.ANY),
-                  pl.BlockSpec(memory_space=pltpu.SMEM)],
+        in_specs=[pl.BlockSpec(memory_space=pltpu.HBM)] * 3,
         out_specs=pl.BlockSpec(memory_space=pl.ANY),
         scratch_shapes=[
             pltpu.VMEM((n_ij, n_cd * n_row), jnp.bfloat16),
@@ -195,7 +228,10 @@
             pltpu.VMEM((n_col, SLOTS, TILE, TILE), jnp.bfloat16),
             pltpu.VMEM((TILE, n_ab), jnp.bfloat16),
             pltpu.VMEM((n_ij, n_ab), jnp.bfloat16),
-            dma((2,)),
+            pltpu.SMEM(sym_mask.shape, jnp.int32),
+            pltpu.SemaphoreType.REGULAR((n_col // 2,)),
+            pltpu.SemaphoreType.REGULAR,
+            dma((3,)),
             dma((CHUNKS,)),
             dma((near, CHUNKS)),
             dma((max(n_row // 2 - 1, 1), CHUNKS)),
@@ -208,7 +244,7 @@
             flops=2 * n_ij * n_ab * n_cd * n_row, bytes_accessed=6 * n_ij * n_ab, transcendentals=0),
         compiler_params=pltpu.CompilerParams(
             collective_id=0, has_side_effects=True, vmem_limit_bytes=48 * 1024 * 1024),
-    )(amplitudes, integrals, sym_mask)
+    )(*(pltpu.with_memory_space_constraint(x, pltpu.HBM) for x in (amplitudes, integrals, sym_mask)))
 
 
 def solution(mesh):

time: 33.1 us -> 25.8 us (0.78)
  Pallas kernels: 28.9 us -> 24.3 us
  local copies, waits for them, and re-layouts: 4 us -> 1.32 us
    pallas_call x1, Pallas kernels: 28.9 us -> 24.3 us  [shards(): pl.pallas_call(functools.partial(kernel, n_row, n_col), out_shape=jax.Sha...]
    unnamed x7 -> x1, local copies, waits for them, and re-layouts: 4 us -> 1.32 us
where the time goes in v2:
time: 25.8 us; the launch traced here: 25.7 us
  Pallas kernels  24.3 us (94%)
  local copies, waits for them, and re-layouts  1.32 us (5%)
    pallas_call x1, Pallas kernels, shards(): pl.pallas_call(functools.partial(kernel, n_row, n_col), out_shape=jax.Sha...  24.3 us
    unnamed x1, local copies, waits for them, and re-layouts  1.32 us

profile of v2, /device:TPU:0, one launch (start us, length us, event | category | flops | bytes accessed | tf_op | source)
XLA Modules:
  0.0 25.7 jit_solution(7462592234680143947)
XLA Ops:
  0.0 24.3 %shard_map.37 = bf16[1024,1024]{1,0:T(8,128)(2,1)S(1)} custom-call(bf16[1024,256]{1,0:T(8,128)(2,1)} %amps.1, bf16[128,1024]{1,0:T(8,128)(2,1)} %ints.1, s32[8,32]{1,0:T(8,128)} %mask_hbm.1), custom_call_target="tpu_custom_call" | custom-call | flops 2147483648 | bytes 6291456 | tf_op jit(solution)/shard_map/pallas_call | solution.py:220
  24.3 1.3 %copy.5 = bf16[1024,1024]{1,0:T(8,128)(2,1)} copy(bf16[1024,1024]{1,0:T(8,128)(2,1)S(1)} %shard_map.37) | data formatting | bytes 4194304

commit v3 on v2

--- a/solution.py
+++ b/solution.py
@@ -9,8 +9,9 @@
 
 TILE = 128
 SLOTS = 2
-CHUNKS = 8
-WINDOW = 4
+CHUNKS = 16
+WINDOW = 5
+GROUPS = ((0, 4, 10), (4, 8, 13), (8, 12, 15), (12, 14, 15), (14, 16, 15))
 MESH = pl.DeviceIdType.MESH
 
 
@@ -127,32 +128,34 @@
         pltpu.make_async_copy(comp.at[source], comp.at[source], v_recv.at[source]).wait()
 
 
-    def build_dense():
-        def one(k, carry):
-            first = comp[k, 0].astype(jnp.float32)
-            second = comp[k, 1].astype(jnp.float32)
+    def build_dense(parity):
+        def one(u, carry):
+            k = 2 * u + parity
+            first, second = comp[k, 0], comp[k, 1]
             w = slot_weights(k)
             for t in range(n_tiles):
                 dense[pl.ds(pl.multiple_of(k * TILE, TILE), TILE), t * TILE:(t + 1) * TILE] = (
-                    first * w[t][0] + second * w[t][1]).astype(jnp.bfloat16)
+                    first * w[t][0].astype(jnp.bfloat16) + second * w[t][1].astype(jnp.bfloat16))
             return carry
-        lax.fori_loop(0, n_col, one, 0)
-
-    def out_copy(c):
-        span = pl.ds(c * step_rows, step_rows)
-        return pltpu.make_async_copy(out_v.at[span], out.at[span], out_sem.at[c])
-
-    def multiply(c):
-        corner = [(i2, j2) for i2 in range(1, ni) for j2 in range(1, nj)]
-        for di, dj in corner:
-            arrive(((i + di) % ni) * nj + (j + dj) % nj, c)
-        span = slice(c * step_rows, (c + 1) * step_rows)
+        lax.fori_loop(0, n_z, one, 0)
+
+    def out_copy(g):
+        span = pl.ds(GROUPS[g][0] * step_rows, (GROUPS[g][1] - GROUPS[g][0]) * step_rows)
+        return pltpu.make_async_copy(out_v.at[span], out.at[span], out_sem.at[g])
+
+    def multiply(g):
+        begin, end, _ = GROUPS[g]
+        for c in range(begin, end):
+            for di in range(1, ni):
+                for dj in range(1, nj):
+                    arrive(((i + di) % ni) * nj + (j + dj) % nj, c)
+        span = slice(begin * step_rows, end * step_rows)
         width = 2 * TILE
         for at in range(0, n_ab, width):
             out_v[span, at:at + width] = jnp.dot(
                 rows_all[span, :], dense[:, at:at + width],
                 preferred_element_type=jnp.float32).astype(jnp.bfloat16)
-        out_copy(c).start()
+        out_copy(g).start()
 
     def take(c):
         copies = forwards(c)
@@ -179,24 +182,21 @@
             def _():
                 pl.semaphore_wait(ready_core, 1)
             sibling_copy(0).start()
-        if c == 3:
+        if c == 5:
             for d, peer in enumerate(peers):
                 v_arrive(2 * peer + core)
                 sibling_copy(d + 1).start()
-        if c == 5:
+        if c == 7:
+            build_dense(core)
+        if c == 8:
             own_copy.wait()
             v_arrive(sibling)
             for peer in peers:
                 v_arrive(2 * peer + 1 - core)
-            build_dense()
-            multiply(0)
-        if c == 6:
-            multiply(1)
-            multiply(2)
-        if c == 7:
-            multiply(3)
-    for c in range(4, CHUNKS):
-        multiply(c)
+            build_dense(1 - core)
+        for g, group in enumerate(GROUPS):
+            if group[2] == c:
+                multiply(g)
 
     for c in range(CHUNKS):
         for d in range(len(near)):
@@ -208,8 +208,8 @@
         v_copy(d).wait_send()
     for d in range(len(peers) + 1):
         sibling_copy(d).wait_send()
-    for c in range(CHUNKS):
-        out_copy(c).wait()
+    for g in range(len(GROUPS)):
+        out_copy(g).wait()
 
 
 def shards(n_row, n_col, amplitudes, integrals, sym_mask):
@@ -232,7 +232,7 @@
             pltpu.SemaphoreType.REGULAR((n_col // 2,)),
             pltpu.SemaphoreType.REGULAR,
             dma((3,)),
-            dma((CHUNKS,)),
+            dma((len(GROUPS),)),
             dma((near, CHUNKS)),
             dma((max(n_row // 2 - 1, 1), CHUNKS)),
             dma((n_row, CHUNKS)),

time: 25.8 us -> 26.9 us (1.043)
  Pallas kernels: 24.3 us -> 25.4 us
    pallas_call x1, Pallas kernels: 24.3 us -> 25.4 us  [shards(): pl.pallas_call(functools.partial(kernel, n_row, n_col), out_shape=jax.Sha...]
where the time goes in v3:
time: 26.9 us; the launch traced here: 26.8 us
  Pallas kernels  25.4 us (94%)
  local copies, waits for them, and re-layouts  1.32 us (5%)
    pallas_call x1, Pallas kernels, shards(): pl.pallas_call(functools.partial(kernel, n_row, n_col), out_shape=jax.Sha...  25.4 us
    unnamed x1, local copies, waits for them, and re-layouts  1.32 us

profile of v3, /device:TPU:0, one launch (start us, length us, event | category | flops | bytes accessed | tf_op | source)
XLA Modules:
  0.0 26.8 jit_solution(10565956901928880248)
XLA Ops:
  0.0 25.4 %shard_map.37 = bf16[1024,1024]{1,0:T(8,128)(2,1)S(1)} custom-call(bf16[1024,256]{1,0:T(8,128)(2,1)} %amps.1, bf16[128,1024]{1,0:T(8,128)(2,1)} %ints.1, s32[8,32]{1,0:T(8,128)} %mask_hbm.1), custom_call_target="tpu_custom_call" | custom-call | flops 2147483648 | bytes 6291456 | tf_op jit(solution)/shard_map/pallas_call | solution.py:220
  25.4 1.3 %copy.5 = bf16[1024,1024]{1,0:T(8,128)(2,1)} copy(bf16[1024,1024]{1,0:T(8,128)(2,1)S(1)} %shard_map.37) | data formatting | bytes 4194304

commit v4 on v3

--- a/solution.py
+++ b/solution.py
@@ -9,9 +9,9 @@
 
 TILE = 128
 SLOTS = 2
-CHUNKS = 16
-WINDOW = 5
-GROUPS = ((0, 4, 10), (4, 8, 13), (8, 12, 15), (12, 14, 15), (14, 16, 15))
+CHUNKS = 8
+WINDOW = 8
+GROUPS = ((0, 2, 7), (2, 4, 7), (4, 6, 7), (6, 7, 7), (7, 8, 7))
 MESH = pl.DeviceIdType.MESH
 
 
@@ -182,13 +182,13 @@
             def _():
                 pl.semaphore_wait(ready_core, 1)
             sibling_copy(0).start()
-        if c == 5:
+        if c == 3:
             for d, peer in enumerate(peers):
                 v_arrive(2 * peer + core)
                 sibling_copy(d + 1).start()
-        if c == 7:
+        if c == 4:
             build_dense(core)
-        if c == 8:
+        if c == 5:
             own_copy.wait()
             v_arrive(sibling)
             for peer in peers:

time: 26.9 us -> 25.2 us (0.937)
  Pallas kernels: 25.4 us -> 23.8 us
    pallas_call x1, Pallas kernels: 25.4 us -> 23.8 us  [shards(): pl.pallas_call(functools.partial(kernel, n_row, n_col), out_shape=jax.Sha...]
where the time goes in v4:
time: 25.2 us; the launch traced here: 25.1 us
  Pallas kernels  23.8 us (94%)
  local copies, waits for them, and re-layouts  1.32 us (5%)
    pallas_call x1, Pallas kernels, shards(): pl.pallas_call(functools.partial(kernel, n_row, n_col), out_shape=jax.Sha...  23.8 us
    unnamed x1, local copies, waits for them, and re-layouts  1.32 us

profile of v4, /device:TPU:0, one launch (start us, length us, event | category | flops | bytes accessed | tf_op | source)
XLA Modules:
  0.0 25.1 jit_solution(9841675520907753886)
XLA Ops:
  0.0 23.8 %shard_map.37 = bf16[1024,1024]{1,0:T(8,128)(2,1)S(1)} custom-call(bf16[1024,256]{1,0:T(8,128)(2,1)} %amps.1, bf16[128,1024]{1,0:T(8,128)(2,1)} %ints.1, s32[8,32]{1,0:T(8,128)} %mask_hbm.1), custom_call_target="tpu_custom_call" | custom-call | flops 2147483648 | bytes 6291456 | tf_op jit(solution)/shard_map/pallas_call | solution.py:220
  23.8 1.3 %copy.5 = bf16[1024,1024]{1,0:T(8,128)(2,1)} copy(bf16[1024,1024]{1,0:T(8,128)(2,1)S(1)} %shard_map.37) | data formatting | bytes 4194304

commit v5 on v4

--- a/solution.py
+++ b/solution.py
@@ -15,8 +15,8 @@
 MESH = pl.DeviceIdType.MESH
 
 
-def kernel(n_row, n_col, amps, ints, mask_hbm, out, rows_all, dense, comp, ints_v, out_v, mask,
-           ready_z, ready_core, local_sem, out_sem, own_send, fwd_send, amp_recv, v_send, v_recv, s_send):
+def kernel(n_row, n_col, amps, ints, mask_hbm, out, rows_all, dense, comp, ints_v, mask,
+           ready_z, ready_core, local_sem, own_send, fwd_send, amp_recv, v_send, v_recv, s_send):
     ni, nj = 2, n_row // 2
     row, col = lax.axis_index("row"), lax.axis_index("col")
     i, j = row // nj, row % nj
@@ -139,10 +139,6 @@
             return carry
         lax.fori_loop(0, n_z, one, 0)
 
-    def out_copy(g):
-        span = pl.ds(GROUPS[g][0] * step_rows, (GROUPS[g][1] - GROUPS[g][0]) * step_rows)
-        return pltpu.make_async_copy(out_v.at[span], out.at[span], out_sem.at[g])
-
     def multiply(g):
         begin, end, _ = GROUPS[g]
         for c in range(begin, end):
@@ -152,10 +148,9 @@
         span = slice(begin * step_rows, end * step_rows)
         width = 2 * TILE
         for at in range(0, n_ab, width):
-            out_v[span, at:at + width] = jnp.dot(
+            out[span, at:at + width] = jnp.dot(
                 rows_all[span, :], dense[:, at:at + width],
                 preferred_element_type=jnp.float32).astype(jnp.bfloat16)
-        out_copy(g).start()
 
     def take(c):
         copies = forwards(c)
@@ -208,8 +203,6 @@
         v_copy(d).wait_send()
     for d in range(len(peers) + 1):
         sibling_copy(d).wait_send()
-    for g in range(len(GROUPS)):
-        out_copy(g).wait()
 
 
 def shards(n_row, n_col, amplitudes, integrals, sym_mask):
@@ -221,18 +214,16 @@
         functools.partial(kernel, n_row, n_col),
         out_shape=jax.ShapeDtypeStruct((n_ij, n_ab), jnp.bfloat16),
         in_specs=[pl.BlockSpec(memory_space=pltpu.HBM)] * 3,
-        out_specs=pl.BlockSpec(memory_space=pl.ANY),
+        out_specs=pl.BlockSpec(memory_space=pltpu.VMEM),
         scratch_shapes=[
             pltpu.VMEM((n_ij, n_cd * n_row), jnp.bfloat16),
             pltpu.VMEM((n_col * TILE, n_ab), jnp.bfloat16),
             pltpu.VMEM((n_col, SLOTS, TILE, TILE), jnp.bfloat16),
             pltpu.VMEM((TILE, n_ab), jnp.bfloat16),
-            pltpu.VMEM((n_ij, n_ab), jnp.bfloat16),
             pltpu.SMEM(sym_mask.shape, jnp.int32),
             pltpu.SemaphoreType.REGULAR((n_col // 2,)),
             pltpu.SemaphoreType.REGULAR,
             dma((3,)),
-            dma((len(GROUPS),)),
             dma((near, CHUNKS)),
             dma((max(n_row // 2 - 1, 1), CHUNKS)),
             dma((n_row, CHUNKS)),

time: 25.2 us -> 25.1 us (level)
  no operation moved by 1% of the time
where the time goes in v5:
time: 25.1 us; the launch traced here: 25 us
  Pallas kernels  23.7 us (94%)
  local copies, waits for them, and re-layouts  1.32 us (5%)
    pallas_call x1, Pallas kernels, shards(): pl.pallas_call(functools.partial(kernel, n_row, n_col), out_shape=jax.Sha...  23.7 us
    unnamed x1, local copies, waits for them, and re-layouts  1.32 us

profile of v5, /device:TPU:0, one launch (start us, length us, event | category | flops | bytes accessed | tf_op | source)
XLA Modules:
  0.0 25.0 jit_solution(1939406399322784725)
XLA Ops:
  0.0 23.7 %shard_map.37 = bf16[1024,1024]{1,0:T(8,128)(2,1)S(1)} custom-call(bf16[1024,256]{1,0:T(8,128)(2,1)} %amps.1, bf16[128,1024]{1,0:T(8,128)(2,1)} %ints.1, s32[8,32]{1,0:T(8,128)} %mask_hbm.1), custom_call_target="tpu_custom_call" | custom-call | flops 2147483648 | bytes 6291456 | tf_op jit(solution)/shard_map/pallas_call | solution.py:213
  23.7 1.3 %copy.5 = bf16[1024,1024]{1,0:T(8,128)(2,1)} copy(bf16[1024,1024]{1,0:T(8,128)(2,1)S(1)} %shard_map.37) | data formatting | bytes 4194304

commit v6 on v5

--- a/solution.py
+++ b/solution.py
@@ -11,11 +11,12 @@
 SLOTS = 2
 CHUNKS = 8
 WINDOW = 8
-GROUPS = ((0, 2, 7), (2, 4, 7), (4, 6, 7), (6, 7, 7), (7, 8, 7))
+GROUPS = ((0, 2), (2, 4), (4, 6))
+LAST = (6, 8)
 MESH = pl.DeviceIdType.MESH
 
 
-def kernel(n_row, n_col, amps, ints, mask_hbm, out, rows_all, dense, comp, ints_v, mask,
+def kernel(n_row, n_col, amps, ints, mask_hbm, out, rows_all, dense, comp, ints_v, partial, mask,
            ready_z, ready_core, local_sem, own_send, fwd_send, amp_recv, v_send, v_recv, s_send):
     ni, nj = 2, n_row // 2
     row, col = lax.axis_index("row"), lax.axis_index("col")
@@ -139,18 +140,32 @@
             return carry
         lax.fori_loop(0, n_z, one, 0)
 
-    def multiply(g):
-        begin, end, _ = GROUPS[g]
+    corner = [((i + di) % ni) * nj + (j + dj) % nj for di in range(1, ni) for dj in range(1, nj)]
+    width = 2 * TILE
+
+    def arrive_corner(begin, end):
         for c in range(begin, end):
-            for di in range(1, ni):
-                for dj in range(1, nj):
-                    arrive(((i + di) % ni) * nj + (j + dj) % nj, c)
+            for source in corner:
+                arrive(source, c)
+
+    def multiply(begin, end):
+        arrive_corner(begin, end)
         span = slice(begin * step_rows, end * step_rows)
-        width = 2 * TILE
         for at in range(0, n_ab, width):
             out[span, at:at + width] = jnp.dot(
                 rows_all[span, :], dense[:, at:at + width],
                 preferred_element_type=jnp.float32).astype(jnp.bfloat16)
+
+    last = slice(LAST[0] * step_rows, LAST[1] * step_rows)
+
+    def last_dot(sources, at):
+        total = None
+        for source in sources:
+            depth = pl.ds(pl.multiple_of(source * n_cd, n_cd), n_cd)
+            product = jnp.dot(rows_all[last, depth], dense[depth, at:at + width],
+                              preferred_element_type=jnp.float32)
+            total = product if total is None else total + product
+        return total
 
     def take(c):
         copies = forwards(c)
@@ -189,9 +204,16 @@
             for peer in peers:
                 v_arrive(2 * peer + 1 - core)
             build_dense(1 - core)
-        for g, group in enumerate(GROUPS):
-            if group[2] == c:
-                multiply(g)
+
+    for begin, end in GROUPS[:-1]:
+        multiply(begin, end)
+    for at in range(0, n_ab, width):
+        partial[:, at:at + width] = last_dot([row] + near, at)
+    multiply(*GROUPS[-1])
+    arrive_corner(*LAST)
+    for at in range(0, n_ab, width):
+        out[last, at:at + width] = (
+            partial[:, at:at + width] + last_dot(corner, at)).astype(jnp.bfloat16)
 
     for c in range(CHUNKS):
         for d in range(len(near)):
@@ -220,6 +242,7 @@
             pltpu.VMEM((n_col * TILE, n_ab), jnp.bfloat16),
             pltpu.VMEM((n_col, SLOTS, TILE, TILE), jnp.bfloat16),
             pltpu.VMEM((TILE, n_ab), jnp.bfloat16),
+            pltpu.VMEM(((LAST[1] - LAST[0]) * n_ij // CHUNKS, n_ab), jnp.float32),
             pltpu.SMEM(sym_mask.shape, jnp.int32),
             pltpu.SemaphoreType.REGULAR((n_col // 2,)),
             pltpu.SemaphoreType.REGULAR,

time: 25.1 us -> 24.6 us (0.980)
  Pallas kernels: 23.7 us -> 23.1 us
    pallas_call x1, Pallas kernels: 23.7 us -> 23.1 us  [shards(): pl.pallas_call(functools.partial(kernel, n_row, n_col), out_shape=jax.Sha...]
where the time goes in v6:
time: 24.6 us; the launch traced here: 24.4 us
  Pallas kernels  23.1 us (94%)
  local copies, waits for them, and re-layouts  1.32 us (5%)
    pallas_call x1, Pallas kernels, shards(): pl.pallas_call(functools.partial(kernel, n_row, n_col), out_shape=jax.Sha...  23.1 us
    unnamed x1, local copies, waits for them, and re-layouts  1.32 us

profile of v6, /device:TPU:0, one launch (start us, length us, event | category | flops | bytes accessed | tf_op | source)
XLA Modules:
  0.0 24.4 jit_solution(115843056646941591)
XLA Ops:
  0.0 23.1 %shard_map.37 = bf16[1024,1024]{1,0:T(8,128)(2,1)S(1)} custom-call(bf16[1024,256]{1,0:T(8,128)(2,1)} %amps.1, bf16[128,1024]{1,0:T(8,128)(2,1)} %ints.1, s32[8,32]{1,0:T(8,128)} %mask_hbm.1), custom_call_target="tpu_custom_call" | custom-call | flops 2147483648 | bytes 6291456 | tf_op jit(solution)/shard_map/pallas_call | solution.py:235
  23.1 1.3 %copy.5 = bf16[1024,1024]{1,0:T(8,128)(2,1)} copy(bf16[1024,1024]{1,0:T(8,128)(2,1)S(1)} %shard_map.37) | data formatting | bytes 4194304

commit v7 on v6

--- a/solution.py
+++ b/solution.py
@@ -9,10 +9,10 @@
 
 TILE = 128
 SLOTS = 2
-CHUNKS = 8
-WINDOW = 8
-GROUPS = ((0, 2), (2, 4), (4, 6))
-LAST = (6, 8)
+CHUNKS = 4
+WINDOW = 4
+GROUPS = ((0, 1), (1, 2), (2, 3))
+LAST = (3, 4)
 MESH = pl.DeviceIdType.MESH
 
 
@@ -192,13 +192,13 @@
             def _():
                 pl.semaphore_wait(ready_core, 1)
             sibling_copy(0).start()
-        if c == 3:
+        if c == 1:
             for d, peer in enumerate(peers):
                 v_arrive(2 * peer + core)
                 sibling_copy(d + 1).start()
-        if c == 4:
+        if c == 1:
             build_dense(core)
-        if c == 5:
+        if c == 2:
             own_copy.wait()
             v_arrive(sibling)
             for peer in peers:

time: 24.6 us -> 25 us (1.016)
  Pallas kernels: 23.1 us -> 23.5 us
    pallas_call x1, Pallas kernels: 23.1 us -> 23.5 us  [shards(): pl.pallas_call(functools.partial(kernel, n_row, n_col), out_shape=jax.Sha...]
where the time goes in v7:
time: 25 us; the launch traced here: 24.9 us
  Pallas kernels  23.5 us (94%)
  local copies, waits for them, and re-layouts  1.32 us (5%)
    pallas_call x1, Pallas kernels, shards(): pl.pallas_call(functools.partial(kernel, n_row, n_col), out_shape=jax.Sha...  23.5 us
    unnamed x1, local copies, waits for them, and re-layouts  1.32 us

profile of v7, /device:TPU:0, one launch (start us, length us, event | category | flops | bytes accessed | tf_op | source)
XLA Modules:
  0.0 24.9 jit_solution(10332769199528777465)
XLA Ops:
  0.0 23.5 %shard_map.37 = bf16[1024,1024]{1,0:T(8,128)(2,1)S(1)} custom-call(bf16[1024,256]{1,0:T(8,128)(2,1)} %amps.1, bf16[128,1024]{1,0:T(8,128)(2,1)} %ints.1, s32[8,32]{1,0:T(8,128)} %mask_hbm.1), custom_call_target="tpu_custom_call" | custom-call | flops 2147483648 | bytes 6291456 | tf_op jit(solution)/shard_map/pallas_call | solution.py:235
  23.5 1.3 %copy.5 = bf16[1024,1024]{1,0:T(8,128)(2,1)} copy(bf16[1024,1024]{1,0:T(8,128)(2,1)S(1)} %shard_map.37) | data formatting | bytes 4194304
